TPU v7x, 32 devices: a whole 2x2x4 slice. The times are simulated.
32 devices in a mesh: section: 2 (over y), expert: 16 (over z, x, core).
Axes of the slice: x: 2, y: 2, z: 4, core: 2. Of those that a mesh axis runs over, the one named last changes fastest.
Arguments:
- inputs_fwd: bfloat16 [3840, 3584], P(('section', 'expert')), may hold values from -6 to 6
- inputs_saved: bfloat16 [3840, 3584], P(('section', 'expert')), may hold values from -6 to 6
- cotangent: bfloat16 [3840, 3584], P(('section', 'expert')), may hold values from -6 to 6
- routes_fwd: int32 [3840, 8], P(('section', 'expert')), may hold values from 0 to 255, as said below
- gates_fwd: float32 [3840, 8], P(('section', 'expert')), may hold values from 0.2 to 1
- routes_bwd: int32 [3840, 8], P(('section', 'expert')), may hold values from 0 to 255, as said below
- gates_bwd: float32 [3840, 8], P(('section', 'expert')), may hold values from 0.2 to 1
- gate_w: bfloat16 [2, 16, 448, 256], P('section', 'expert'), may hold values from -0.09375 to 0.09375
- up_w: bfloat16 [2, 16, 448, 256], P('section', 'expert'), may hold values from -0.09375 to 0.09375
- down_w: bfloat16 [2, 16, 448, 256], P('section', 'expert'), may hold values from -0.1875 to 0.1875
Outputs:
- forward_next: bfloat16 [3840, 3584], P(('section', 'expert'))
- gradient_next: bfloat16 [3840, 3584], P(('section', 'expert'))
Inputs may be any that keep to these rules, and one draw needn't show every extreme that they name: `routes_fwd`: each token names 8 different experts. Among the 120 tokens of one device, each expert below 1 is named by 1 to 8 tokens; one such expert is named by exactly 8 tokens on every device. `routes_bwd`: as for routes_fwd.
All inputs are finite; a program needn't handle non-finite values.
Results may differ from a plain program's by a relative error of at most 0.0034.
Values may be sent and summed in bfloat16 or wider, within the bound.
A program may use at most 64 MiB of HBM per device.

v0:
```python
import jax
import jax.numpy as jnp
from jax import lax
from jax.sharding import PartitionSpec as P

CAP = 8


def from_partner(array, axis, distance):
    return lax.ppermute(array, axis, [(i, i ^ 1 << distance) for i in range(lax.axis_size(axis))])


def as_sent(array):
    return jax.tree.map(lambda a: a.astype(jnp.bfloat16) if a.dtype == jnp.float32 else a, array)


def shifted(block, axis, distance):
    devices = range(lax.axis_size(axis))
    route = [((i - distance) % len(devices), i) for i in devices]
    return lax.ppermute(block, axis, route)


def tables(routes, gates, flight, capacity):
    experts_range = jnp.arange(flight, dtype=jnp.int32)
    matches = routes[:, :, None] == experts_range[None, None, :]
    member = jnp.any(matches, axis=1)
    weight_sum = jnp.sum(jnp.where(matches, gates[:, :, None], jnp.float32(0.0)), axis=1)
    position = jnp.cumsum(member.astype(jnp.int32), axis=0) - 1
    slots_range = jnp.arange(capacity, dtype=jnp.int32)
    chosen = member[:, :, None] & (position[:, :, None] == slots_range[None, None, :])
    picker = jnp.transpose(chosen, (1, 2, 0)).astype(jnp.float32)
    return (picker, weight_sum)


def spread(rows):
    flight, capacity, width = rows.shape
    grouped = rows.reshape(flight, 4, capacity // 4, width)
    copies = jnp.broadcast_to(grouped[:, None], (flight, 4, 4, capacity // 4, width))
    return copies.reshape(flight * 16, capacity // 4, width)


def collect(returned):
    total, quarter, width = returned.shape
    flight = total // 16
    summed = jnp.sum(returned.reshape(flight, 4, 4, quarter, width).astype(jnp.float32), axis=1)
    return summed.reshape(flight * 4 * quarter, width)


def ordered(first, second, flag):
    joined = []
    for one, two in zip(first, second):
        low_high = jnp.concatenate([one, two], axis=0)
        high_low = jnp.concatenate([two, one], axis=0)
        joined.append(jnp.where(flag == 0, low_high, high_low))
    return tuple(joined)


def expert_forward(rows, weights):
    wg, wu, wdt = weights
    contract = (((1,), (1,)), ((), ()))
    pre_gate = jnp.dot(rows, wg, preferred_element_type=jnp.float32)
    pre_up = jnp.dot(rows, wu, preferred_element_type=jnp.float32)
    hidden = (jax.nn.silu(pre_gate) * pre_up).astype(jnp.bfloat16)
    return lax.dot_general(hidden, wdt, contract, preferred_element_type=jnp.float32).astype(
        jnp.bfloat16
    )


def expert_backward(rows, upstream, weights):
    wg, wu, wdt = weights
    contract = (((1,), (1,)), ((), ()))
    pre_gate = jnp.dot(rows, wg, preferred_element_type=jnp.float32)
    pre_up = jnp.dot(rows, wu, preferred_element_type=jnp.float32)
    sigma = jax.nn.sigmoid(pre_gate)
    activ = pre_gate * sigma
    slope = sigma * (1.0 + pre_gate * (1.0 - sigma))
    d_hidden = jnp.dot(upstream, wdt, preferred_element_type=jnp.float32)
    d_gate = (d_hidden * pre_up * slope).astype(jnp.bfloat16)
    d_up = (d_hidden * activ).astype(jnp.bfloat16)
    summed = lax.dot_general(d_gate, wg, contract, preferred_element_type=jnp.float32)
    summed = summed + lax.dot_general(d_up, wu, contract, preferred_element_type=jnp.float32)
    return summed.astype(jnp.bfloat16)


def per_device(
    inputs_fwd,
    inputs_saved,
    cotangent,
    routes_fwd,
    gates_fwd,
    routes_bwd,
    gates_bwd,
    gate_w,
    up_w,
    down_w,
):
    flight = lax.axis_size("expert") // 16
    low_bit = lax.axis_index("expert") % 2
    high_bit = lax.axis_index("expert") // 2 % 2
    core_bit = lax.axis_index("section") % 2
    own = (gate_w[0, 0], up_w[0, 0], down_w[0, 0])
    first = from_partner((own[0], own[1], own[2]), "expert", 0)
    step_one = ordered(own, first, low_bit)
    second = jax.tree.map(
        lambda part, own: part.astype(own.dtype),
        from_partner(as_sent(step_one), "expert", 1),
        step_one,
    )
    step_two = ordered(step_one, second, high_bit)
    third = jax.tree.map(
        lambda part, own: part.astype(own.dtype),
        from_partner(as_sent(step_two), "section", 0),
        step_two,
    )
    weights = ordered(step_two, third, core_bit)
    pick_fwd, weight_fwd = tables(routes_fwd, gates_fwd, flight, CAP)
    pick_bwd, weight_bwd = tables(routes_bwd, gates_bwd, flight, CAP)
    rows_fwd = jnp.einsum(
        "wst,td->wsd", pick_fwd.astype(jnp.bfloat16), inputs_fwd, preferred_element_type=jnp.float32
    ).astype(jnp.bfloat16)
    rows_bwd = jnp.einsum(
        "wst,td->wsd",
        pick_bwd.astype(jnp.bfloat16),
        inputs_saved,
        preferred_element_type=jnp.float32,
    ).astype(jnp.bfloat16)
    scaled = pick_bwd * jnp.transpose(weight_bwd)[:, None, :]
    upstream = jnp.einsum(
        "wst,td->wsd", scaled, cotangent.astype(jnp.float32), precision=lax.Precision.HIGHEST
    ).astype(jnp.bfloat16)
    send_fwd = spread(rows_fwd)
    send_rows = spread(rows_bwd)
    send_up = spread(upstream)
    received = lax.all_to_all(send_fwd, "expert", split_axis=0, concat_axis=0, tiled=True)
    width = received.shape[-1]
    result = expert_forward(received.reshape(-1, width), weights).reshape(received.shape)
    back_fwd = lax.all_to_all(result, "expert", split_axis=0, concat_axis=0, tiled=True)
    saved_rows = lax.all_to_all(send_rows, "expert", split_axis=0, concat_axis=0, tiled=True)
    grad_rows = lax.all_to_all(send_up, "expert", split_axis=0, concat_axis=0, tiled=True)
    width = saved_rows.shape[-1]
    result = expert_backward(saved_rows.reshape(-1, width), grad_rows.reshape(-1, width), weights)
    back_bwd = lax.all_to_all(
        result.reshape(saved_rows.shape), "expert", split_axis=0, concat_axis=0, tiled=True
    )
    tokens_here = inputs_fwd.shape[0]
    mix_fwd = (pick_fwd * jnp.transpose(weight_fwd)[:, None, :]).reshape(-1, tokens_here)
    branch = jnp.einsum("mt,md->td", mix_fwd, collect(back_fwd), precision=lax.Precision.HIGHEST)
    layer_out = (inputs_fwd.astype(jnp.float32) + branch).astype(jnp.bfloat16)
    carried = jnp.einsum(
        "mt,md->td",
        pick_bwd.reshape(-1, tokens_here),
        collect(back_bwd),
        precision=lax.Precision.HIGHEST,
    )
    input_grad = (cotangent.astype(jnp.float32) + carried).astype(jnp.bfloat16)
    onward = shifted(layer_out, "section", 1)
    forward_next = shifted(onward, "section", 1)
    backward = shifted(input_grad, "section", -1)
    gradient_next = shifted(backward, "section", -1)
    return (forward_next, gradient_next)


def solution(mesh):
    placed = (
        P(("section", "expert"), None),
        P(("section", "expert"), None),
        P(("section", "expert"), None),
        P(("section", "expert"), None),
        P(("section", "expert"), None),
        P(("section", "expert"), None),
        P(("section", "expert"), None),
        P("section", "expert", None, None),
        P("section", "expert", None, None),
        P("section", "expert", None, None),
    )
    return jax.shard_map(
        per_device,
        mesh=mesh,
        in_specs=placed,
        out_specs=(P(("section", "expert"), None), P(("section", "expert"), None)),
        check_vma=False,
    )
```

profile of v0, /device:TPU:0, one launch (start us, length us, event | category | flops | bytes accessed | tf_op | source)
XLA Modules:
  0.0 222.9 jit_solution(9007090091048620649)
XLA Ops:
  4.8 7.4 %all-to-all-start = ((bf16[16,2,3584]{2,1,0:T(2,128)(2,1)}), bf16[16,2,3584]{2,1,0:T(2,128)(2,1)S(1)}, u32[]{:S(2)}, u32[]{:S(2)}) async-start(bf16[16,2,3584]{2,1,0:T(2,128)(2,1)} %bitcast.5), calls=%async_computation | async-start | bytes 458752 | tf_op jit(solution)/shard_map/all_to_all | solution.py:134
  14.7 1.7 collective-permute-start.1
  16.5 5.3 %all-to-all-done = bf16[16,2,3584]{2,1,0:T(2,128)(2,1)S(1)} async-done(((bf16[16,2,3584]{2,1,0:T(2,128)(2,1)}), bf16[16,2,3584]{2,1,0:T(2,128)(2,1)S(1)}, u32[]{:S(2)}, u32[]{:S(2)}) %all-to-all-start) | async-done | bytes 229408 | tf_op jit(solution)/shard_map/all_to_all | solution.py:134
  22.5 3.5 %all-to-all-start.3 = ((bf16[16,2,3584]{2,1,0:T(2,128)(2,1)}), bf16[16,2,3584]{2,1,0:T(2,128)(2,1)S(1)}, u32[]{:S(2)}, u32[]{:S(2)}) async-start(bf16[16,2,3584]{2,1,0:T(2,128)(2,1)} %bitcast.16), calls=%async_computation.3 | async-start | bytes 458752 | tf_op jit(solution)/shard_map/all_to_all | solution.py:138
  28.1 1.9 collective-permute-start.4
  30.0 5.6 %all-to-all-done.3 = bf16[16,2,3584]{2,1,0:T(2,128)(2,1)S(1)} async-done(((bf16[16,2,3584]{2,1,0:T(2,128)(2,1)}), bf16[16,2,3584]{2,1,0:T(2,128)(2,1)S(1)}, u32[]{:S(2)}, u32[]{:S(2)}) %all-to-all-start.3) | async-done | bytes 229408 | tf_op jit(solution)/shard_map/all_to_all | solution.py:138
  36.4 4.2 %all-to-all-start.2 = ((bf16[16,2,3584]{2,1,0:T(2,128)(2,1)}), bf16[16,2,3584]{2,1,0:T(2,128)(2,1)}, u32[]{:S(2)}, u32[]{:S(2)}) async-start(bf16[16,2,3584]{2,1,0:T(2,128)(2,1)} %bitcast.14), calls=%async_computation.2 | async-start | bytes 458752 | tf_op jit(solution)/shard_map/all_to_all | solution.py:139
  45.0 1.8 collective-permute-start.7
  48.5 1.7 reshape.305
  54.8 3.3 %collective-permute-done.7 = bf16[896,256]{1,0:T(8,128)(2,1)} collective-permute-done((bf16[896,256]{1,0:T(8,128)(2,1)S(1)}, bf16[896,256]{1,0:T(8,128)(2,1)}, u32[]{:S(2)}, u32[]{:S(2)}) %collective-permute-start.7) | collective-permute-done | bytes 458784 | tf_op jit(solution)/shard_map/ppermute | solution.py:10
  60.3 5.1 %collective-permute-done.2 = bf16[1792,256]{1,0:T(8,128)(2,1)} collective-permute-done((bf16[1792,256]{1,0:T(8,128)(2,1)S(1)}, bf16[1792,256]{1,0:T(8,128)(2,1)}, u32[]{:S(2)}, u32[]{:S(2)}) %collective-permute-start.2) | collective-permute-done | bytes 917536 | tf_op jit(solution)/shard_map/ppermute | solution.py:10
  65.3 1.9 maximum_select_fusion
  69.4 15.5 %collective-permute-done.5 = bf16[1792,256]{1,0:T(8,128)(2,1)S(1)} collective-permute-done((bf16[1792,256]{1,0:T(8,128)(2,1)S(1)}, bf16[1792,256]{1,0:T(8,128)(2,1)S(1)}, u32[]{:S(2)}, u32[]{:S(2)}) %collective-permute-start.5) | collective-permute-done | bytes 917536 | tf_op jit(solution)/shard_map/ppermute | solution.py:10
  85.9 18.1 %collective-permute-done.8 = bf16[1792,256]{1,0:T(8,128)(2,1)} collective-permute-done((bf16[1792,256]{1,0:T(8,128)(2,1)S(1)}, bf16[1792,256]{1,0:T(8,128)(2,1)}, u32[]{:S(2)}, u32[]{:S(2)}) %collective-permute-start.8) | collective-permute-done | bytes 917536 | tf_op jit(solution)/shard_map/ppermute | solution.py:10
  104.0 5.3 %convolution_convert_fusion = bf16[32,3584]{1,0:T(8,128)(2,1)} fusion(bf16[1792,256]{1,0:T(8,128)(2,1)} %collective-permute-done.8, bf16[1792,256]{1,0:T(8,128)(2,1)} %copy-done.9, pred[]{:T(512)S(6)} %eq.73, f32[32,256]{1,0:T(8,128)} %fusion.52, bf16[32,3584]{1,0:T(8,128)(2,1)} %reshape.298, bf16[1792,256]{1,0:T(8,128)(2,1)} %copy-done.26, ...), kind=kOutput, calls=%fused_computation.6 | convolution fusion | flops 134119424 | bytes 4161537 | tf_op jit(solution)/shard_map/dot_general | solution.py:64
  111.0 5.9 %all-to-all-start.1 = ((bf16[16,2,3584]{2,1,0:T(2,128)(2,1)}), bf16[16,2,3584]{2,1,0:T(2,128)(2,1)}, u32[]{:S(2)}, u32[]{:S(2)}) async-start(bf16[16,2,3584]{2,1,0:T(2,128)(2,1)} %reshape.299), calls=%async_computation.1 | async-start | bytes 458752 | tf_op jit(solution)/shard_map/all_to_all | solution.py:137
  116.9 2.8 %fusion.5 = f32[32,256]{1,0:T(8,128)S(1)} fusion(bf16[32,3584]{1,0:T(8,128)(2,1)} %reshape.303, bf16[1792,256]{1,0:T(8,128)(2,1)} %collective-permute-done.8, bf16[1792,256]{1,0:T(8,128)(2,1)} %copy-done.9, pred[]{:T(512)S(6)} %eq.73), kind=kOutput, calls=%fused_computation.24 | convolution fusion | flops 66977792 | bytes 2097153 | tf_op jit(solution)/shard_map/dot_general | solution.py:77
  121.8 4.4 %fusion.2 = bf16[32,3584]{1,0:T(8,128)(2,1)} fusion(f32[32,3584]{1,0:T(8,128)} %fusion.10, bf16[3584,256]{1,0:T(8,128)(2,1)S(1)} %maximum_select_fusion, f32[32,256]{1,0:T(8,128)} %copy-done.28, bf16[32,3584]{1,0:T(8,128)(2,1)} %reshape.305, f32[32,256]{1,0:T(8,128)} %fusion.53, bf16[1792,256]{1,0:T(8,128)(2,1)} %copy-done.26, ...), kind=kOutput, calls=%fused_computation.5 | convolution fusion | flops 126009344 | bytes 4653057 | tf_op jit(solution)/shard_map/dot_general | solution.py:80
  127.9 6.1 %all-to-all-start.4 = ((bf16[16,2,3584]{2,1,0:T(2,128)(2,1)}), bf16[16,2,3584]{2,1,0:T(2,128)(2,1)S(1)}, u32[]{:S(2)}, u32[]{:S(2)}) async-start(bf16[16,2,3584]{2,1,0:T(2,128)(2,1)} %reshape.306), calls=%async_computation.4 | async-start | bytes 458752 | tf_op jit(solution)/shard_map/all_to_all | solution.py:142
  135.3 8.2 %all-to-all-done.4 = bf16[16,2,3584]{2,1,0:T(2,128)(2,1)S(1)} async-done(((bf16[16,2,3584]{2,1,0:T(2,128)(2,1)}), bf16[16,2,3584]{2,1,0:T(2,128)(2,1)S(1)}, u32[]{:S(2)}, u32[]{:S(2)}) %all-to-all-start.4) | async-done | bytes 229408 | tf_op jit(solution)/shard_map/all_to_all | solution.py:142
  148.6 18.3 %collective-permute-done.11 = bf16[120,3584]{1,0:T(8,128)(2,1)S(1)} collective-permute-done((bf16[120,3584]{1,0:T(8,128)(2,1)S(1)}, bf16[120,3584]{1,0:T(8,128)(2,1)S(1)}, u32[]{:S(2)}, u32[]{:S(2)}) %collective-permute-start.11) | collective-permute-done | bytes 860192 | tf_op jit(solution)/shard_map/ppermute | solution.py:20
  168.4 16.9 %collective-permute-done.9 = bf16[120,3584]{1,0:T(8,128)(2,1)S(1)} collective-permute-done((bf16[120,3584]{1,0:T(8,128)(2,1)S(1)}, bf16[120,3584]{1,0:T(8,128)(2,1)S(1)}, u32[]{:S(2)}, u32[]{:S(2)}) %collective-permute-start.9) | collective-permute-done | bytes 860192 | tf_op jit(solution)/shard_map/ppermute | solution.py:20
  186.9 16.9 %collective-permute-done.12 = bf16[120,3584]{1,0:T(8,128)(2,1)S(1)} collective-permute-done((bf16[120,3584]{1,0:T(8,128)(2,1)S(1)}, bf16[120,3584]{1,0:T(8,128)(2,1)S(1)}, u32[]{:S(2)}, u32[]{:S(2)}) %collective-permute-start.12) | collective-permute-done | bytes 860192 | tf_op jit(solution)/shard_map/ppermute | solution.py:20
  203.8 17.3 %collective-permute-done.10 = bf16[120,3584]{1,0:T(8,128)(2,1)S(1)} collective-permute-done((bf16[120,3584]{1,0:T(8,128)(2,1)S(1)}, bf16[120,3584]{1,0:T(8,128)(2,1)S(1)}, u32[]{:S(2)}, u32[]{:S(2)}) %collective-permute-start.10) | collective-permute-done | bytes 860192 | tf_op jit(solution)/shard_map/ppermute | solution.py:20
  (117 shorter events, 42.6 us)
Async XLA Ops:
  4.0 22.8 %copy-start.3 = (bf16[120,3584]{1,0:T(8,128)(2,1)S(1)}, bf16[120,3584]{1,0:T(8,128)(2,1)}, u32[]{:S(2)}) copy-start(bf16[120,3584]{1,0:T(8,128)(2,1)} %param.12) | copy-start | bytes 2580484
  4.8 16.9 %all-to-all-start = ((bf16[16,2,3584]{2,1,0:T(2,128)(2,1)}), bf16[16,2,3584]{2,1,0:T(2,128)(2,1)S(1)}, u32[]{:S(2)}, u32[]{:S(2)}) async-start(bf16[16,2,3584]{2,1,0:T(2,128)(2,1)} %bitcast.5), calls=%async_computation | async-start | bytes 458752 | tf_op jit(solution)/shard_map/all_to_all | solution.py:134
  12.2 2.3 %collective-permute-start = (bf16[448,256]{1,0:T(8,128)(2,1)S(1)}, bf16[448,256]{1,0:T(8,128)(2,1)S(1)}, u32[]{:S(2)}, u32[]{:S(2)}) collective-permute-start(bf16[448,256]{1,0:T(8,128)(2,1)S(1)} %bitcast.58), channel_id=1, source_target_pairs={{0,1},{1,0},{2,3},{3,2},{4,5},{5,4},{6,7},{7,6},{8,9},{9,8},{10,11... | collective-permute-start | bytes 688136 | tf_op jit(solution)/shard_map/ppermute | solution.py:10
  12.7 15.2 %collective-permute-start.3 = (bf16[448,256]{1,0:T(8,128)(2,1)S(1)}, bf16[448,256]{1,0:T(8,128)(2,1)S(1)}, u32[]{:S(2)}, u32[]{:S(2)}) collective-permute-start(bf16[448,256]{1,0:T(8,128)(2,1)S(1)} %bitcast.60), channel_id=1, source_target_pairs={{0,1},{1,0},{2,3},{3,2},{4,5},{5,4},{6,7},{7,6},{8,9},{9,8},{10,11... | collective-permute-start | bytes 688136 | tf_op jit(solution)/shard_map/ppermute | solution.py:10
  12.8 30.8 %collective-permute-start.6 = (bf16[448,256]{1,0:T(8,128)(2,1)}, bf16[448,256]{1,0:T(8,128)(2,1)}, u32[]{:S(2)}, u32[]{:S(2)}) collective-permute-start(bf16[448,256]{1,0:T(8,128)(2,1)} %bitcast.8), channel_id=1, source_target_pairs={{0,1},{1,0},{2,3},{3,2},{4,5},{5,4},{6,7},{7,6},{8,9},{9,8},{10,11... | collective-permute-start | bytes 688136 | tf_op jit(solution)/shard_map/ppermute | solution.py:10
  14.7 25.9 %collective-permute-start.1 = (bf16[896,256]{1,0:T(8,128)(2,1)S(1)}, bf16[896,256]{1,0:T(8,128)(2,1)}, u32[]{:S(2)}, u32[]{:S(2)}) collective-permute-start(bf16[896,256]{1,0:T(8,128)(2,1)S(1)} %maximum_select_fusion.6), channel_id=1, source_target_pairs={{0,2},{1,3},{2,0},{3,1},{4,6},{5,7},{6,4},{7,5},{8,10},{9,11},{10,... | collective-permute-start | bytes 1376264 | tf_op jit(solution)/shard_map/ppermute | solution.py:10
  22.5 13.0 %all-to-all-start.3 = ((bf16[16,2,3584]{2,1,0:T(2,128)(2,1)}), bf16[16,2,3584]{2,1,0:T(2,128)(2,1)S(1)}, u32[]{:S(2)}, u32[]{:S(2)}) async-start(bf16[16,2,3584]{2,1,0:T(2,128)(2,1)} %bitcast.16), calls=%async_computation.3 | async-start | bytes 458752 | tf_op jit(solution)/shard_map/all_to_all | solution.py:138
  28.1 23.8 %collective-permute-start.4 = (bf16[896,256]{1,0:T(8,128)(2,1)S(1)}, bf16[896,256]{1,0:T(8,128)(2,1)}, u32[]{:S(2)}, u32[]{:S(2)}) collective-permute-start(bf16[896,256]{1,0:T(8,128)(2,1)S(1)} %maximum_select_fusion.7), channel_id=1, source_target_pairs={{0,2},{1,3},{2,0},{3,1},{4,6},{5,7},{6,4},{7,5},{8,10},{9,11},{10,... | collective-permute-start | bytes 1376264 | tf_op jit(solution)/shard_map/ppermute | solution.py:10
  36.4 13.8 %all-to-all-start.2 = ((bf16[16,2,3584]{2,1,0:T(2,128)(2,1)}), bf16[16,2,3584]{2,1,0:T(2,128)(2,1)}, u32[]{:S(2)}, u32[]{:S(2)}) async-start(bf16[16,2,3584]{2,1,0:T(2,128)(2,1)} %bitcast.14), calls=%async_computation.2 | async-start | bytes 458752 | tf_op jit(solution)/shard_map/all_to_all | solution.py:139
  42.0 23.4 %collective-permute-start.2 = (bf16[1792,256]{1,0:T(8,128)(2,1)S(1)}, bf16[1792,256]{1,0:T(8,128)(2,1)}, u32[]{:S(2)}, u32[]{:S(2)}) collective-permute-start(bf16[1792,256]{1,0:T(8,128)(2,1)S(1)} %maximum_select_fusion.3), channel_id=1, source_target_pairs={{0,16},{16,0},{1,17},{17,1},{2,18},{18,2},{3,19},{19,3},{4,20},{20... | collective-permute-start | bytes 2752520 | tf_op jit(solution)/shard_map/ppermute | solution.py:10
  45.0 13.2 %collective-permute-start.7 = (bf16[896,256]{1,0:T(8,128)(2,1)S(1)}, bf16[896,256]{1,0:T(8,128)(2,1)}, u32[]{:S(2)}, u32[]{:S(2)}) collective-permute-start(bf16[896,256]{1,0:T(8,128)(2,1)S(1)} %maximum_select_fusion.8), channel_id=1, source_target_pairs={{0,2},{1,3},{2,0},{3,1},{4,6},{5,7},{6,4},{7,5},{8,10},{9,11},{10,... | collective-permute-start | bytes 1376264 | tf_op jit(solution)/shard_map/ppermute | solution.py:10
  53.3 31.6 %collective-permute-start.5 = (bf16[1792,256]{1,0:T(8,128)(2,1)S(1)}, bf16[1792,256]{1,0:T(8,128)(2,1)S(1)}, u32[]{:S(2)}, u32[]{:S(2)}) collective-permute-start(bf16[1792,256]{1,0:T(8,128)(2,1)S(1)} %maximum_select_fusion.4), channel_id=1, source_target_pairs={{0,16},{16,0},{1,17},{17,1},{2,18},{18,2},{3,19},{19,3},{4,20},{20... | collective-permute-start | bytes 2752520 | tf_op jit(solution)/shard_map/ppermute | solution.py:10
  59.6 44.4 %collective-permute-start.8 = (bf16[1792,256]{1,0:T(8,128)(2,1)S(1)}, bf16[1792,256]{1,0:T(8,128)(2,1)}, u32[]{:S(2)}, u32[]{:S(2)}) collective-permute-start(bf16[1792,256]{1,0:T(8,128)(2,1)S(1)} %maximum_select_fusion.5), channel_id=1, source_target_pairs={{0,16},{16,0},{1,17},{17,1},{2,18},{18,2},{3,19},{19,3},{4,20},{20... | collective-permute-start | bytes 2752520 | tf_op jit(solution)/shard_map/ppermute | solution.py:10
  111.0 16.9 %all-to-all-start.1 = ((bf16[16,2,3584]{2,1,0:T(2,128)(2,1)}), bf16[16,2,3584]{2,1,0:T(2,128)(2,1)}, u32[]{:S(2)}, u32[]{:S(2)}) async-start(bf16[16,2,3584]{2,1,0:T(2,128)(2,1)} %reshape.299), calls=%async_computation.1 | async-start | bytes 458752 | tf_op jit(solution)/shard_map/all_to_all | solution.py:137
  126.2 17.7 %copy-start.18 = (pred[120]{0:T(512)(128)(4,1)S(1)}, pred[120]{0:T(512)(128)(4,1)}, u32[]{:S(2)}) copy-start(pred[120]{0:T(512)(128)(4,1)} %copy-done.17) | copy-start | bytes 364
  127.9 18.5 %copy-start.4 = (bf16[120,3584]{1,0:T(8,128)(2,1)S(1)}, bf16[120,3584]{1,0:T(8,128)(2,1)}, u32[]{:S(2)}) copy-start(bf16[120,3584]{1,0:T(8,128)(2,1)} %param.10) | copy-start | bytes 2580484
  127.9 18.5 %copy-start.20 = (s32[120]{0:T(128)S(1)}, s32[120]{0:T(128)}, u32[]{:S(2)}) copy-start(s32[120]{0:T(128)} %copy-done.19) | copy-start | bytes 1444
  127.9 18.5 %copy-start.22 = (pred[120]{0:T(512)(128)(4,1)S(1)}, pred[120]{0:T(512)(128)(4,1)}, u32[]{:S(2)}) copy-start(pred[120]{0:T(512)(128)(4,1)} %copy-done.21) | copy-start | bytes 364
  127.9 18.5 %copy-start.25 = (f32[120]{0:T(128)S(1)}, f32[120]{0:T(128)}, u32[]{:S(2)}) copy-start(f32[120]{0:T(128)} %get-tuple-element.4) | copy-start | bytes 1444
  127.9 15.6 %all-to-all-start.4 = ((bf16[16,2,3584]{2,1,0:T(2,128)(2,1)}), bf16[16,2,3584]{2,1,0:T(2,128)(2,1)S(1)}, u32[]{:S(2)}, u32[]{:S(2)}) async-start(bf16[16,2,3584]{2,1,0:T(2,128)(2,1)} %reshape.306), calls=%async_computation.4 | async-start | bytes 458752 | tf_op jit(solution)/shard_map/all_to_all | solution.py:142
  144.8 22.1 %collective-permute-start.11 = (bf16[120,3584]{1,0:T(8,128)(2,1)S(1)}, bf16[120,3584]{1,0:T(8,128)(2,1)S(1)}, u32[]{:S(2)}, u32[]{:S(2)}) collective-permute-start(bf16[120,3584]{1,0:T(8,128)(2,1)S(1)} %fusion.1), channel_id=1, source_target_pairs={{16,0},{0,16},{17,1},{1,17},{18,2},{2,18},{19,3},{3,19},{20,4},{4,... | collective-permute-start | bytes 2580488 | tf_op jit(solution)/shard_map/ppermute | solution.py:20
  148.0 37.3 %collective-permute-start.9 = (bf16[120,3584]{1,0:T(8,128)(2,1)S(1)}, bf16[120,3584]{1,0:T(8,128)(2,1)S(1)}, u32[]{:S(2)}, u32[]{:S(2)}) collective-permute-start(bf16[120,3584]{1,0:T(8,128)(2,1)S(1)} %fusion), channel_id=1, source_target_pairs={{16,0},{0,16},{17,1},{1,17},{18,2},{2,18},{19,3},{3,19},{20,4},{4,... | collective-permute-start | bytes 2580488 | tf_op jit(solution)/shard_map/ppermute | solution.py:20
  166.9 36.9 %collective-permute-start.12 = (bf16[120,3584]{1,0:T(8,128)(2,1)S(1)}, bf16[120,3584]{1,0:T(8,128)(2,1)S(1)}, u32[]{:S(2)}, u32[]{:S(2)}) collective-permute-start(bf16[120,3584]{1,0:T(8,128)(2,1)S(1)} %collective-permute-done.11), channel_id=1, source_target_pairs={{16,0},{0,16},{17,1},{1,17},{18,2},{2,18},{19,3},{3,19},{20,4},{4,... | collective-permute-start | bytes 2580488 | tf_op jit(solution)/shard_map/ppermute | solution.py:20
  185.3 35.7 %collective-permute-start.10 = (bf16[120,3584]{1,0:T(8,128)(2,1)S(1)}, bf16[120,3584]{1,0:T(8,128)(2,1)S(1)}, u32[]{:S(2)}, u32[]{:S(2)}) collective-permute-start(bf16[120,3584]{1,0:T(8,128)(2,1)S(1)} %collective-permute-done.9), channel_id=1, source_target_pairs={{16,0},{0,16},{17,1},{1,17},{18,2},{2,18},{19,3},{3,19},{20,4},{4,... | collective-permute-start | bytes 2580488 | tf_op jit(solution)/shard_map/ppermute | solution.py:20
  (23 other events, 170.8 us)
where the time goes:
time: 224 us; the launch traced here: 223 us
  waiting for transfers between devices  131 us (58%)
  starting transfers between devices  42.4 us (19%)
  matrix products  21.2 us (9%)
  local copies, waits for them, and re-layouts  15.2 us (7%)
  other arithmetic  12.4 us (6%)
    ppermute x4, waiting for transfers between devices, shifted(): return lax.ppermute(block, axis, route)  69.4 us
    ppermute x9, waiting for transfers between devices, from_partner(): lax.ppermute(array, axis, [(i, i ^ 1 << distance) for i in range(lax.axis...  42 us
    ppermute x9, starting transfers between devices, from_partner(): lax.ppermute(array, axis, [(i, i ^ 1 << distance) for i in range(lax.axis...  10.2 us
    all_to_all x1, waiting for transfers between devices, per_device(): lax.all_to_all(result.reshape(saved_rows.shape), 'expert', split_axis=0,...  8.21 us
    select_n x7, other arithmetic, ordered(): joined.append(jnp.where(flag == 0, low_high, high_low))  7.83 us
    all_to_all x1, starting transfers between devices, per_device(): lax.all_to_all(send_fwd, 'expert', split_axis=0, concat_axis=0, tiled=True)  7.36 us
    all_to_all x1, starting transfers between devices, per_device(): lax.all_to_all(result.reshape(saved_rows.shape), 'expert', split_axis=0,...  6.11 us
    all_to_all x1, starting transfers between devices, per_device(): lax.all_to_all(result, 'expert', split_axis=0, concat_axis=0, tiled=True)  5.87 us
  transfers between devices with their start and end apart: 18, of which 11 were waited for; matrix products, arithmetic and copies ran while one was open for 15% of the time, Pallas kernels for 0%

commit v1 on v0

v1 whole, which is shorter than its diff:
```python
import functools

import jax
import jax.numpy as jnp
from jax import lax
from jax.experimental import pallas as pl
from jax.experimental.pallas import tpu as pltpu
from jax.sharding import PartitionSpec as P

CAP = 8
SLICES = 4
HID = 256
MESH = pl.DeviceIdType.MESH
F32 = jnp.float32
BF16 = jnp.bfloat16
NT = (((1,), (1,)), ((), ()))


def member_of(routes, gates, e, width):
    tokens = routes.shape[0]
    match = routes == e
    member = jnp.max(match.astype(F32), axis=1, keepdims=True)
    masked = jnp.where(match, gates, 0.0)
    tri = (
        lax.broadcasted_iota(jnp.int32, (tokens, tokens), 0)
        >= lax.broadcasted_iota(jnp.int32, (tokens, tokens), 1)
    ).astype(F32).astype(BF16)
    wide = jnp.broadcast_to(member, (tokens, width)).astype(BF16)
    position = jnp.dot(tri, wide, preferred_element_type=F32) - 1.0
    slot = (lax.broadcasted_iota(jnp.int32, (tokens, width), 1) % CAP).astype(F32)
    chosen = jnp.where((position == slot) & (wide > 0), 1.0, 0.0)
    return chosen, masked


def transposed(chosen):
    eye = (
        lax.broadcasted_iota(jnp.int32, (CAP, CAP), 0)
        == lax.broadcasted_iota(jnp.int32, (CAP, CAP), 1)
    ).astype(F32).astype(BF16)
    return lax.dot_general(eye, chosen.astype(BF16), NT, preferred_element_type=F32)


def kernel(
    n_expert, chunk,
    x_ref, s_ref, g_ref, rf_ref, gf_ref, rb_ref, gb_ref, gw_ref, uw_ref, dw_ref,
    of_ref, ob_ref,
    send_f, send_b, in_f, in_b, w, p32_f, p32_b, ps_f, ps_b, pr_f, pr_b, h_f, h_b,
    o_f, o_b, r_f, r_b,
    w_s, w_r, inf_s, inf_r, inb_s, inb_r, pf_s, pf_r, pb_s, pb_r, hf_s, hf_r, hb_s, hb_r,
    of_s, of_r, ob_s, ob_r,
):
    flight = n_expert // 16
    group = n_expert
    half = group // 2
    rows = group // 4 * CAP
    section, expert = lax.axis_index("section"), lax.axis_index("expert")
    layer, c, k = section // 2, section % 2, expert % 2
    place = expert // 2
    me = c * half + place
    x = place % 2
    h = place // 2 % 4
    e_here = place // 8
    q = 2 * c + x

    def device(n):
        return (layer * 2 + n // half, (n % half) * 2 + k)

    def quad_device(other):
        return (layer * 2 + other // 2, e_here * 16 + h * 4 + (other % 2) * 2 + k)

    partner = (section, expert + 1 - 2 * k)

    barrier = pltpu.get_barrier_semaphore()
    pl.semaphore_signal(barrier, inc=1, device_id=partner, device_id_type=MESH)

    def greet(d, carry):
        pl.semaphore_signal(
            barrier, inc=1, device_id=device((me + d) % group), device_id_type=MESH
        )
        return carry

    lax.fori_loop(1, group, greet, 0)

    def scatter(src, dst, ssem, rsem):
        def body(d, carry):
            n = (me + d) % group
            spot = n % half
            pltpu.make_async_remote_copy(
                src_ref=src(n, spot // 8, 2 * (n // half) + spot % 2),
                dst_ref=dst, send_sem=ssem.at[n], recv_sem=rsem.at[me],
                device_id=device(n), device_id_type=MESH,
            ).start()
            return carry

        lax.fori_loop(1, group, body, 0)

    def gathered(src, dst, ssem, rsem):
        def body(d, carry):
            n = (me + d) % group
            pltpu.make_async_remote_copy(
                src_ref=src, dst_ref=dst(n), send_sem=ssem.at[n], recv_sem=rsem.at[n],
                device_id=device(n), device_id_type=MESH,
            ).wait_recv()
            return carry

        lax.fori_loop(1, group, body, 0)

    def drained(src, dst, ssem, rsem):
        def body(d, carry):
            n = (me + d) % group
            pltpu.make_async_remote_copy(
                src_ref=src, dst_ref=dst, send_sem=ssem.at[n], recv_sem=rsem.at[n],
                device_id=device(n), device_id_type=MESH,
            ).wait_send()
            return carry

        lax.fori_loop(1, group, body, 0)

    def quad_copy(src, dst, ssem, rsem, d):
        return pltpu.make_async_remote_copy(
            src_ref=src, dst_ref=dst, send_sem=ssem.at[d], recv_sem=rsem.at[d],
            device_id=quad_device((q + d) % 4), device_id_type=MESH,
        )

    for e in range(flight):
        chosen, _ = member_of(rf_ref[...], gf_ref[...], e, CAP)
        pick = transposed(chosen).astype(BF16)
        for part in range(4):
            cols = slice(part * chunk, (part + 1) * chunk)
            send_f[e, part] = jnp.dot(pick, x_ref[:, cols], preferred_element_type=F32).astype(BF16)

    pl.semaphore_wait(barrier, group)
    scatter(lambda n, e, part: send_f.at[e, part], in_f.at[me], inf_s, inf_r)
    weight_copies = []
    for i, ref in enumerate((gw_ref, uw_ref, dw_ref)):
        copy = pltpu.make_async_remote_copy(
            src_ref=ref.at[0, 0], dst_ref=w.at[i, k], send_sem=w_s.at[i], recv_sem=w_r.at[i],
            device_id=partner, device_id_type=MESH,
        )
        copy.start()
        weight_copies.append(copy)

    for e in range(flight):
        chosen, masked = member_of(rb_ref[...], gb_ref[...], e, CAP)
        pick_f32 = transposed(chosen)
        pick = pick_f32.astype(BF16)
        weight = lax.dot_general(
            jnp.ones((CAP, masked.shape[1]), F32), masked, NT,
            precision=lax.Precision.HIGHEST, preferred_element_type=F32,
        )
        gate = jnp.sum(pick_f32 * weight, axis=1, keepdims=True)
        for part in range(4):
            cols = slice(part * chunk, (part + 1) * chunk)
            send_b[e, part, 0] = jnp.dot(pick, s_ref[:, cols], preferred_element_type=F32).astype(BF16)
            picked = jnp.dot(pick, g_ref[:, cols], preferred_element_type=F32)
            send_b[e, part, 1] = (picked * gate).astype(BF16)
    scatter(lambda n, e, part: send_b.at[e, part], in_b.at[me], inb_s, inb_r)

    in_f[me] = send_f[e_here, q]
    in_b[me] = send_b[e_here, q]
    for i, ref in enumerate((gw_ref, uw_ref, dw_ref)):
        w[i, k] = ref[0, 0]
    for copy in weight_copies:
        copy.wait_recv()

    def matrix(i):
        return w[i].reshape(chunk, HID)

    def flat(block):
        return block.astype(F32).reshape(group * CAP, chunk).astype(BF16)

    def reduce_part(p32, ps, pr, ssem, rsem):
        copies = [quad_copy(ps.at[(q + d) % 4], pr.at[d], ssem, rsem, d) for d in range(1, 4)]
        for copy in copies:
            copy.start()
        total = p32[q]
        for d in range(1, 4):
            copies[d - 1].wait_recv()
            total = total + pr[d].astype(F32)
        return total, copies

    def share(h_ref, value, ssem, rsem):
        h_ref[q] = value
        copies = [quad_copy(h_ref.at[q], h_ref.at[q], ssem, rsem, d) for d in range(1, 4)]
        for copy in copies:
            copy.start()
        for d in range(1, 4):
            quad_copy(h_ref.at[q], h_ref.at[(q - d + 4) % 4], ssem, rsem, d).wait_recv()
        return copies

    gathered(send_f.at[0, 0], lambda n: in_f.at[n], inf_s, inf_r)
    block = flat(in_f[...])
    for i in range(2):
        part = jnp.dot(block, matrix(i), preferred_element_type=F32).reshape(4, rows, HID)
        p32_f[:, :, i * HID:(i + 1) * HID] = part
        ps_f[:, :, i * HID:(i + 1) * HID] = part.astype(BF16)
    total, sent_pf = reduce_part(p32_f, ps_f, pr_f, pf_s, pf_r)
    a, b = total[:, :HID], total[:, HID:]
    sent_hf = share(h_f, (a * jax.nn.sigmoid(a) * b).astype(BF16), hf_s, hf_r)
    hidden = h_f[...].reshape(group * CAP, HID)
    o_f[...] = (
        lax.dot_general(hidden, matrix(2), NT, preferred_element_type=F32)
        .reshape(group, CAP, chunk).astype(BF16)
    )
    scatter(lambda n, e, part: o_f.at[n], r_f.at[c, e_here, h, x], of_s, of_r)
    r_f[c, e_here, h, x] = o_f[me]

    gathered(send_b.at[0, 0], lambda n: in_b.at[n], inb_s, inb_r)
    block = flat(in_b[:, 0])
    for i in range(3):
        if i == 2:
            block = flat(in_b[:, 1])
        part = jnp.dot(block, matrix(i), preferred_element_type=F32).reshape(4, rows, HID)
        p32_b[:, :, i * HID:(i + 1) * HID] = part
        ps_b[:, :, i * HID:(i + 1) * HID] = part.astype(BF16)
    total, sent_pb = reduce_part(p32_b, ps_b, pr_b, pb_s, pb_r)
    a, b, d_hidden = total[:, :HID], total[:, HID:2 * HID], total[:, 2 * HID:]
    sigma = jax.nn.sigmoid(a)
    d_gate = (d_hidden * b * (sigma * (1.0 + a * (1.0 - sigma)))).astype(BF16)
    d_up = (d_hidden * (a * sigma)).astype(BF16)
    sent_hb = share(h_b, jnp.concatenate([d_gate, d_up], axis=1), hb_s, hb_r)
    both = h_b[...].reshape(group * CAP, 2 * HID)
    back = lax.dot_general(both[:, :HID], matrix(0), NT, preferred_element_type=F32)
    back = back + lax.dot_general(both[:, HID:], matrix(1), NT, preferred_element_type=F32)
    o_b[...] = back.reshape(group, CAP, chunk).astype(BF16)
    scatter(lambda n, e, part: o_b.at[n], r_b.at[c, e_here, h, x], ob_s, ob_r)
    r_b[c, e_here, h, x] = o_b[me]

    def combine(routes, gates, base, returned, out, weighted):
        picks = []
        for e in range(flight):
            chosen, masked = member_of(routes[...], gates[...], e, SLICES * CAP)
            picks.append((chosen.astype(BF16), jnp.sum(masked, axis=1, keepdims=True)))
        for part in range(4):
            cols = slice(part * chunk, (part + 1) * chunk)
            total = base[:, cols].astype(F32)
            for e in range(flight):
                chosen, weight = picks[e]
                piece = returned[part // 2, e, :, part % 2].astype(F32)
                piece = piece.reshape(SLICES * CAP, chunk).astype(BF16)
                term = jnp.dot(chosen, piece, preferred_element_type=F32)
                total = total + (term * weight if weighted else term)
            out[:, cols] = total.astype(BF16)

    def slot_of(buffer):
        return lambda n: buffer.at[n // half, n % half // 8, n % half // 2 % 4, n % 2]

    gathered(o_f.at[0], slot_of(r_f), of_s, of_r)
    combine(rf_ref, gf_ref, x_ref, r_f, of_ref, True)
    gathered(o_b.at[0], slot_of(r_b), ob_s, ob_r)
    combine(rb_ref, gb_ref, g_ref, r_b, ob_ref, False)

    drained(send_f.at[0, 0], in_f.at[0], inf_s, inf_r)
    drained(send_b.at[0, 0], in_b.at[0], inb_s, inb_r)
    drained(o_f.at[0], r_f.at[0, 0, 0, 0], of_s, of_r)
    drained(o_b.at[0], r_b.at[0, 0, 0, 0], ob_s, ob_r)
    for copy in weight_copies + sent_pf + sent_hf + sent_pb + sent_hb:
        copy.wait_send()


def solution(mesh):
    n_expert, n_section = mesh.shape["expert"], mesh.shape["section"]
    flight, group = n_expert // 16, n_expert
    tokens_spec = P(("section", "expert"), None)
    weight_spec = P("section", "expert", None, None)

    def per_device(*args):
        x = args[0]
        chunk = x.shape[1] // 4
        rows = group // 4 * CAP
        vmem = pl.BlockSpec(memory_space=pltpu.VMEM)
        dma = pltpu.SemaphoreType.DMA
        scratch = [
            pltpu.VMEM((flight, 4, CAP, chunk), BF16),
            pltpu.VMEM((flight, 4, 2, CAP, chunk), BF16),
            pltpu.VMEM((group, CAP, chunk), BF16),
            pltpu.VMEM((group, 2, CAP, chunk), BF16),
            pltpu.VMEM((3, 2, chunk // 2, HID), BF16),
            pltpu.VMEM((4, rows, 2 * HID), F32),
            pltpu.VMEM((4, rows, 3 * HID), F32),
            pltpu.VMEM((4, rows, 2 * HID), BF16),
            pltpu.VMEM((4, rows, 3 * HID), BF16),
            pltpu.VMEM((4, rows, 2 * HID), BF16),
            pltpu.VMEM((4, rows, 3 * HID), BF16),
            pltpu.VMEM((4, rows, HID), BF16),
            pltpu.VMEM((4, rows, 2 * HID), BF16),
            pltpu.VMEM((group, CAP, chunk), BF16),
            pltpu.VMEM((group, CAP, chunk), BF16),
            pltpu.VMEM((2, flight, SLICES, 2, CAP, chunk), BF16),
            pltpu.VMEM((2, flight, SLICES, 2, CAP, chunk), BF16),
            dma((3,)), dma((3,)),
            dma((group,)), dma((group,)), dma((group,)), dma((group,)),
            dma((4,)), dma((4,)), dma((4,)), dma((4,)),
            dma((4,)), dma((4,)), dma((4,)), dma((4,)),
            dma((group,)), dma((group,)), dma((group,)), dma((group,)),
        ]
        out = jax.ShapeDtypeStruct(x.shape, BF16)
        forward, gradient = pl.pallas_call(
            functools.partial(kernel, n_expert, chunk),
            out_shape=(out, out),
            in_specs=[vmem] * 10,
            out_specs=(vmem, vmem),
            scratch_shapes=scratch,
            compiler_params=pltpu.CompilerParams(
                collective_id=0, has_side_effects=True, vmem_limit_bytes=48 * 1024 * 1024
            ),
        )(*args)
        if n_section > 2:
            onward = [(i, (i + 2) % n_section) for i in range(n_section)]
            back = [(i, (i - 2) % n_section) for i in range(n_section)]
            forward = lax.ppermute(forward, "section", onward)
            gradient = lax.ppermute(gradient, "section", back)
        return forward, gradient

    return jax.shard_map(
        per_device,
        mesh=mesh,
        in_specs=(tokens_spec,) * 7 + (weight_spec,) * 3,
        out_specs=(tokens_spec, tokens_spec),
        check_vma=False,
    )
```

time: 224 us -> 54.6 us (0.24)
  waiting for transfers between devices: 131 us -> 0 us
  Pallas kernels: 0 us -> 43.2 us
  starting transfers between devices: 42.4 us -> 0 us
  matrix products: 21.2 us -> 0 us
  other arithmetic: 12.4 us -> 0 us
  local copies, waits for them, and re-layouts: 15.2 us -> 10.3 us
    ppermute x13 -> x0, waiting for transfers between devices: 111 us -> none  [the longest x4 69.4 us: shifted(): return lax.ppermute(block, axis, route)]
    pallas_call x0 -> x1, Pallas kernels: none -> 43.2 us  [per_device(): pl.pallas_call(functools.partial(kernel, n_expert, chunk), out_shape=(out...]
    all_to_all x5 -> x0, starting transfers between devices: 27.1 us -> none  [the longest x1 7.36 us: per_device(): lax.all_to_all(send_fwd, 'expert', split_axis=0, concat_axis=0, tiled=True)]
    dot_general x11 -> x0, matrix products: 21.2 us -> none  [the longest x1 5.34 us: expert_forward(): lax.dot_general(hidden, wdt, contract, preferred_element_type=jnp.float32)]
    all_to_all x5 -> x0, waiting for transfers between devices: 19.1 us -> none  [the longest x1 8.21 us: per_device(): lax.all_to_all(result.reshape(saved_rows.shape), 'expert', split_axis=0,...]
    ppermute x13 -> x0, starting transfers between devices: 15.4 us -> none  [the longest x9 10.2 us: from_partner(): lax.ppermute(array, axis, [(i, i ^ 1 << distance) for i in range(lax.axis...]
    reshape x7 -> x0, local copies, waits for them, and re-layouts: 8.73 us -> none  [the longest x1 1.73 us: per_device(): saved_rows.reshape(-1, width)]
    select_n x7 -> x0, other arithmetic: 7.83 us -> none  [ordered(): joined.append(jnp.where(flag == 0, low_high, high_low))]
  transfers between devices with their start and end apart: 18 -> 0, of which waited for: 11 -> 0; matrix products, arithmetic and copies ran while one was open for 15% -> 0% of each run, Pallas kernels for 0% -> 0%
where the time goes in v1:
time: 54.6 us; the launch traced here: 54.2 us
  Pallas kernels  43.2 us (79%)
  local copies, waits for them, and re-layouts  10.3 us (19%)
  between operations  0.66 us (1%)
    pallas_call x1, Pallas kernels, per_device(): pl.pallas_call(functools.partial(kernel, n_expert, chunk), out_shape=(out...  43.2 us
    unnamed x18, local copies, waits for them, and re-layouts  10.3 us

profile of v1, /device:TPU:0, one launch (start us, length us, event | category | flops | bytes accessed | tf_op | source)
XLA Modules:
  0.0 54.2 jit_solution(4399825796341577188)
XLA Ops:
  0.6 0.0 copy-start.3
  0.6 0.8 %copy.12.rf_ref = s32[120,8]{1,0:T(8,128)S(1)} copy(s32[120,8]{0,1:T(8,128)} %param.13) | data formatting | bytes 7680 | tf_op args[3]
  1.5 0.8 %copy.13.gf_ref = f32[120,8]{1,0:T(8,128)S(1)} copy(f32[120,8]{0,1:T(8,128)} %param.14) | data formatting | bytes 7680 | tf_op args[4]
  2.3 0.8 %copy.14.rb_ref = s32[120,8]{1,0:T(8,128)S(1)} copy(s32[120,8]{0,1:T(8,128)} %param.15) | data formatting | bytes 7680 | tf_op args[5]
  3.0 0.8 %copy.15.gb_ref = f32[120,8]{1,0:T(8,128)S(1)} copy(f32[120,8]{0,1:T(8,128)} %param.16) | data formatting | bytes 7680 | tf_op args[6]
  3.8 0.0 copy-done.3
  3.8 0.0 copy-start
  3.8 1.1 %copy-done = bf16[120,3584]{1,0:T(8,128)(2,1)S(1)} copy-done((bf16[120,3584]{1,0:T(8,128)(2,1)S(1)}, bf16[120,3584]{1,0:T(8,128)(2,1)}, u32[]{:S(2)}) %copy-start) | copy-done | bytes 860184
  5.0 0.0 copy-start.1
  5.0 1.2 %copy-done.1 = bf16[120,3584]{1,0:T(8,128)(2,1)S(1)} copy-done((bf16[120,3584]{1,0:T(8,128)(2,1)S(1)}, bf16[120,3584]{1,0:T(8,128)(2,1)}, u32[]{:S(2)}) %copy-start.1) | copy-done | bytes 860184
  6.1 0.0 copy-start.2
  6.1 1.2 %copy-done.2 = bf16[120,3584]{1,0:T(8,128)(2,1)S(1)} copy-done((bf16[120,3584]{1,0:T(8,128)(2,1)S(1)}, bf16[120,3584]{1,0:T(8,128)(2,1)}, u32[]{:S(2)}) %copy-start.2) | copy-done | bytes 860184
  7.3 0.0 copy-start.4
  7.3 0.9 %copy-done.4 = bf16[1,1,448,256]{3,2,1,0:T(8,128)(2,1)S(1)} copy-done((bf16[1,1,448,256]{3,2,1,0:T(8,128)(2,1)S(1)}, bf16[1,1,448,256]{3,2,1,0:T(8,128)(2,1)}, u32[]{:S(2)}) %copy-start.4) | copy-done | bytes 229400
  8.2 0.0 copy-start.5
  8.2 0.9 %copy-done.5 = bf16[1,1,448,256]{3,2,1,0:T(8,128)(2,1)S(1)} copy-done((bf16[1,1,448,256]{3,2,1,0:T(8,128)(2,1)S(1)}, bf16[1,1,448,256]{3,2,1,0:T(8,128)(2,1)}, u32[]{:S(2)}) %copy-start.5) | copy-done | bytes 229400
  9.2 43.2 %shard_map.113 = (bf16[120,3584]{1,0:T(8,128)(2,1)S(1)}, bf16[120,3584]{1,0:T(8,128)(2,1)S(1)}) custom-call(bf16[120,3584]{1,0:T(8,128)(2,1)S(1)} %copy-done, bf16[120,3584]{1,0:T(8,128)(2,1)S(1)} %copy-done.1, bf16[120,3584]{1,0:T(8,128)(2,1)S(1)} %copy-done.2, s32[120,8]{1,0:T(8,128)S(1)} %copy.12.rf_ref, f32[120,8]{1,0:T(8,128)S(1)} %copy.13.gf_ref, ...), custom_call_target="tpu_custom_call" | custom-call | tf_op jit(solution)/shard_map/pallas_call | solution.py:298
  52.4 0.9 %copy.18 = bf16[120,3584]{1,0:T(8,128)(2,1)} copy(bf16[120,3584]{1,0:T(8,128)(2,1)S(1)} %get-tuple-element.4) | data formatting | bytes 1720320
  53.3 0.9 %copy.19 = bf16[120,3584]{1,0:T(8,128)(2,1)} copy(bf16[120,3584]{1,0:T(8,128)(2,1)S(1)} %get-tuple-element.5) | data formatting | bytes 1720320
Async XLA Ops:
  0.6 3.2 %copy-start.3 = (bf16[1,1,448,256]{3,2,1,0:T(8,128)(2,1)S(1)}, bf16[1,1,448,256]{3,2,1,0:T(8,128)(2,1)}, u32[]{:S(2)}) copy-start(bf16[1,1,448,256]{3,2,1,0:T(8,128)(2,1)} %gw_ref.1) | copy-start | bytes 688132
  3.8 1.2 %copy-start = (bf16[120,3584]{1,0:T(8,128)(2,1)S(1)}, bf16[120,3584]{1,0:T(8,128)(2,1)}, u32[]{:S(2)}) copy-start(bf16[120,3584]{1,0:T(8,128)(2,1)} %x_ref.1) | copy-start | bytes 2580484
  5.0 1.2 %copy-start.1 = (bf16[120,3584]{1,0:T(8,128)(2,1)S(1)}, bf16[120,3584]{1,0:T(8,128)(2,1)}, u32[]{:S(2)}) copy-start(bf16[120,3584]{1,0:T(8,128)(2,1)} %s_ref.1) | copy-start | bytes 2580484
  6.1 1.2 %copy-start.2 = (bf16[120,3584]{1,0:T(8,128)(2,1)S(1)}, bf16[120,3584]{1,0:T(8,128)(2,1)}, u32[]{:S(2)}) copy-start(bf16[120,3584]{1,0:T(8,128)(2,1)} %g_ref.1) | copy-start | bytes 2580484
  7.3 0.9 %copy-start.4 = (bf16[1,1,448,256]{3,2,1,0:T(8,128)(2,1)S(1)}, bf16[1,1,448,256]{3,2,1,0:T(8,128)(2,1)}, u32[]{:S(2)}) copy-start(bf16[1,1,448,256]{3,2,1,0:T(8,128)(2,1)} %uw_ref.1) | copy-start | bytes 688132
  8.2 0.9 %copy-start.5 = (bf16[1,1,448,256]{3,2,1,0:T(8,128)(2,1)S(1)}, bf16[1,1,448,256]{3,2,1,0:T(8,128)(2,1)}, u32[]{:S(2)}) copy-start(bf16[1,1,448,256]{3,2,1,0:T(8,128)(2,1)} %dw_ref.1) | copy-start | bytes 688132

commit v2 on v1

--- a/solution.py
+++ b/solution.py
@@ -16,34 +16,34 @@
 NT = (((1,), (1,)), ((), ()))
 
 
-def member_of(routes, gates, e, width):
-    tokens = routes.shape[0]
-    match = routes == e
-    member = jnp.max(match.astype(F32), axis=1, keepdims=True)
-    masked = jnp.where(match, gates, 0.0)
+def eye(size, dtype):
+    rows = lax.broadcasted_iota(jnp.int32, (size, size), 0)
+    cols = lax.broadcasted_iota(jnp.int32, (size, size), 1)
+    return (rows == cols).astype(F32).astype(dtype)
+
+
+def chosen_of(routes, e, height):
+    tokens = routes.shape[1]
+    member = jnp.max((routes == e).astype(F32), axis=0, keepdims=True)
     tri = (
         lax.broadcasted_iota(jnp.int32, (tokens, tokens), 0)
         >= lax.broadcasted_iota(jnp.int32, (tokens, tokens), 1)
     ).astype(F32).astype(BF16)
-    wide = jnp.broadcast_to(member, (tokens, width)).astype(BF16)
-    position = jnp.dot(tri, wide, preferred_element_type=F32) - 1.0
-    slot = (lax.broadcasted_iota(jnp.int32, (tokens, width), 1) % CAP).astype(F32)
-    chosen = jnp.where((position == slot) & (wide > 0), 1.0, 0.0)
-    return chosen, masked
-
-
-def transposed(chosen):
-    eye = (
-        lax.broadcasted_iota(jnp.int32, (CAP, CAP), 0)
-        == lax.broadcasted_iota(jnp.int32, (CAP, CAP), 1)
-    ).astype(F32).astype(BF16)
-    return lax.dot_general(eye, chosen.astype(BF16), NT, preferred_element_type=F32)
+    wide = jnp.broadcast_to(member, (height, tokens))
+    position = lax.dot_general(wide.astype(BF16), tri, NT, preferred_element_type=F32) - 1.0
+    slot = (lax.broadcasted_iota(jnp.int32, (height, tokens), 0) % CAP).astype(F32)
+    return jnp.where((position == slot) & (wide > 0), 1.0, 0.0)
+
+
+def gate_of(routes, gates, e):
+    return jnp.sum(jnp.where(routes == e, gates, 0.0), axis=0, keepdims=True)
 
 
 def kernel(
     n_expert, chunk,
-    x_ref, s_ref, g_ref, rf_ref, gf_ref, rb_ref, gb_ref, gw_ref, uw_ref, dw_ref,
-    of_ref, ob_ref,
+    x_hbm, s_hbm, g_hbm, rf_hbm, gf_hbm, rb_hbm, gb_hbm, gw_ref, uw_ref, dw_ref,
+    of_hbm, ob_hbm,
+    x_ref, s_ref, g_ref, rf_ref, gf_ref, rb_ref, gb_ref, load, of_ref, ob_ref, store,
     send_f, send_b, in_f, in_b, w, p32_f, p32_b, ps_f, ps_b, pr_f, pr_b, h_f, h_b,
     o_f, o_b, r_f, r_b,
     w_s, w_r, inf_s, inf_r, inb_s, inb_r, pf_s, pf_r, pb_s, pb_r, hf_s, hf_r, hb_s, hb_r,
@@ -68,6 +68,18 @@
     def quad_device(other):
         return (layer * 2 + other // 2, e_here * 16 + h * 4 + (other % 2) * 2 + k)
 
+    loads = [
+        pltpu.make_async_copy(src, dst, load.at[i])
+        for i, (src, dst) in enumerate((
+            (rf_hbm, rf_ref), (x_hbm, x_ref), (rb_hbm, rb_ref), (gb_hbm, gb_ref),
+            (s_hbm, s_ref), (g_hbm, g_ref), (gf_hbm, gf_ref),
+            (gw_ref.at[0, 0], w.at[0, k]), (uw_ref.at[0, 0], w.at[1, k]),
+            (dw_ref.at[0, 0], w.at[2, k]),
+        ))
+    ]
+    for copy in loads:
+        copy.start()
+
     partner = (section, expert + 1 - 2 * k)
 
     barrier = pltpu.get_barrier_semaphore()
@@ -122,9 +134,11 @@
             device_id=quad_device((q + d) % 4), device_id_type=MESH,
         )
 
+    loads[0].wait()
+    picks_f = [chosen_of(rf_ref[...], e, CAP).astype(BF16) for e in range(flight)]
+    loads[1].wait()
     for e in range(flight):
-        chosen, _ = member_of(rf_ref[...], gf_ref[...], e, CAP)
-        pick = transposed(chosen).astype(BF16)
+        pick = picks_f[e]
         for part in range(4):
             cols = slice(part * chunk, (part + 1) * chunk)
             send_f[e, part] = jnp.dot(pick, x_ref[:, cols], preferred_element_type=F32).astype(BF16)
@@ -140,14 +154,12 @@
         copy.start()
         weight_copies.append(copy)
 
+    for copy in loads[2:6]:
+        copy.wait()
     for e in range(flight):
-        chosen, masked = member_of(rb_ref[...], gb_ref[...], e, CAP)
-        pick_f32 = transposed(chosen)
+        pick_f32 = chosen_of(rb_ref[...], e, CAP)
         pick = pick_f32.astype(BF16)
-        weight = lax.dot_general(
-            jnp.ones((CAP, masked.shape[1]), F32), masked, NT,
-            precision=lax.Precision.HIGHEST, preferred_element_type=F32,
-        )
+        weight = gate_of(rb_ref[...], gb_ref[...], e)
         gate = jnp.sum(pick_f32 * weight, axis=1, keepdims=True)
         for part in range(4):
             cols = slice(part * chunk, (part + 1) * chunk)
@@ -158,8 +170,8 @@
 
     in_f[me] = send_f[e_here, q]
     in_b[me] = send_b[e_here, q]
-    for i, ref in enumerate((gw_ref, uw_ref, dw_ref)):
-        w[i, k] = ref[0, 0]
+    for copy in loads[6:]:
+        copy.wait()
     for copy in weight_copies:
         copy.wait_recv()
 
@@ -226,11 +238,20 @@
     scatter(lambda n, e, part: o_b.at[n], r_b.at[c, e_here, h, x], ob_s, ob_r)
     r_b[c, e_here, h, x] = o_b[me]
 
-    def combine(routes, gates, base, returned, out, weighted):
+    def combine(routes, gates, base, returned, out, out_hbm, weighted):
         picks = []
+        stores = []
         for e in range(flight):
-            chosen, masked = member_of(routes[...], gates[...], e, SLICES * CAP)
-            picks.append((chosen.astype(BF16), jnp.sum(masked, axis=1, keepdims=True)))
+            tokens = routes.shape[1]
+            chosen = chosen_of(routes[...], e, SLICES * CAP).astype(BF16)
+            chosen = lax.dot_general(eye(tokens, BF16), chosen, NT, preferred_element_type=F32)
+            gate = None
+            if weighted:
+                gate = lax.dot_general(
+                    eye(tokens, F32), jnp.broadcast_to(gate_of(routes[...], gates[...], e), (CAP, tokens)),
+                    NT, precision=lax.Precision.HIGHEST, preferred_element_type=F32,
+                )[:, :1]
+            picks.append((chosen.astype(BF16), gate))
         for part in range(4):
             cols = slice(part * chunk, (part + 1) * chunk)
             total = base[:, cols].astype(F32)
@@ -241,14 +262,19 @@
                 term = jnp.dot(chosen, piece, preferred_element_type=F32)
                 total = total + (term * weight if weighted else term)
             out[:, cols] = total.astype(BF16)
+            stores.append(pltpu.make_async_copy(
+                out.at[:, cols], out_hbm.at[:, cols], store.at[0 if weighted else 1, part]
+            ))
+            stores[-1].start()
+        return stores
 
     def slot_of(buffer):
         return lambda n: buffer.at[n // half, n % half // 8, n % half // 2 % 4, n % 2]
 
     gathered(o_f.at[0], slot_of(r_f), of_s, of_r)
-    combine(rf_ref, gf_ref, x_ref, r_f, of_ref, True)
+    stores = combine(rf_ref, gf_ref, x_ref, r_f, of_ref, of_hbm, True)
     gathered(o_b.at[0], slot_of(r_b), ob_s, ob_r)
-    combine(rb_ref, gb_ref, g_ref, r_b, ob_ref, False)
+    stores += combine(rb_ref, gb_ref, g_ref, r_b, ob_ref, ob_hbm, False)
 
     drained(send_f.at[0, 0], in_f.at[0], inf_s, inf_r)
     drained(send_b.at[0, 0], in_b.at[0], inb_s, inb_r)
@@ -256,6 +282,8 @@
     drained(o_b.at[0], r_b.at[0, 0, 0, 0], ob_s, ob_r)
     for copy in weight_copies + sent_pf + sent_hf + sent_pb + sent_hb:
         copy.wait_send()
+    for copy in stores:
+        copy.wait()
 
 
 def solution(mesh):
@@ -266,11 +294,16 @@
 
     def per_device(*args):
         x = args[0]
+        args = args[:3] + tuple(a.T for a in args[3:7]) + args[7:]
         chunk = x.shape[1] // 4
         rows = group // 4 * CAP
-        vmem = pl.BlockSpec(memory_space=pltpu.VMEM)
+        hbm = pl.BlockSpec(memory_space=pltpu.HBM)
         dma = pltpu.SemaphoreType.DMA
         scratch = [
+            pltpu.VMEM(x.shape, BF16), pltpu.VMEM(x.shape, BF16), pltpu.VMEM(x.shape, BF16),
+            *[pltpu.VMEM(a.shape, a.dtype) for a in args[3:7]],
+            dma((10,)),
+            pltpu.VMEM(x.shape, BF16), pltpu.VMEM(x.shape, BF16), dma((2, 4)),
             pltpu.VMEM((flight, 4, CAP, chunk), BF16),
             pltpu.VMEM((flight, 4, 2, CAP, chunk), BF16),
             pltpu.VMEM((group, CAP, chunk), BF16),
@@ -298,11 +331,11 @@
         forward, gradient = pl.pallas_call(
             functools.partial(kernel, n_expert, chunk),
             out_shape=(out, out),
-            in_specs=[vmem] * 10,
-            out_specs=(vmem, vmem),
+            in_specs=[hbm] * 10,
+            out_specs=(hbm, hbm),
             scratch_shapes=scratch,
             compiler_params=pltpu.CompilerParams(
-                collective_id=0, has_side_effects=True, vmem_limit_bytes=48 * 1024 * 1024
+                collective_id=0, has_side_effects=True, vmem_limit_bytes=58 * 1024 * 1024
             ),
         )(*args)
         if n_section > 2:

time: 54.6 us -> 47 us (0.86)
  local copies, waits for them, and re-layouts: 10.3 us -> 3.1 us
    unnamed x18 -> x4, local copies, waits for them, and re-layouts: 10.3 us -> 3.1 us
where the time goes in v2:
time: 47 us; the launch traced here: 46.8 us
  Pallas kernels  43 us (91%)
  local copies, waits for them, and re-layouts  3.1 us (7%)
  between operations  0.65 us (1%)
    pallas_call x1, Pallas kernels, per_device(): pl.pallas_call(functools.partial(kernel, n_expert, chunk), out_shape=(out...  43 us
    unnamed x4, local copies, waits for them, and re-layouts  3.1 us

profile of v2, /device:TPU:0, one launch (start us, length us, event | category | flops | bytes accessed | tf_op | source)
XLA Modules:
  0.0 46.8 jit_solution(1458709028491305534)
XLA Ops:
  0.6 43.0 %shard_map.113 = (bf16[120,3584]{1,0:T(8,128)(2,1)}, bf16[120,3584]{1,0:T(8,128)(2,1)}) custom-call(bf16[120,3584]{1,0:T(8,128)(2,1)} %x_hbm.1, bf16[120,3584]{1,0:T(8,128)(2,1)} %s_hbm.1, bf16[120,3584]{1,0:T(8,128)(2,1)} %g_hbm.1, s32[8,120]{1,0:T(8,128)} %bitcast.4, f32[8,120]{1,0:T(8,128)} %bitcast.5, s32[8,120]{1,0:T(8,128)} %bitcast.6, ...), custom_call_target="tpu_custom_call" | custom-call | tf_op jit(solution)/shard_map/pallas_call | solution.py:331
  43.7 0.0 copy-start
  43.7 2.2 %copy.14 = bf16[120,3584]{1,0:T(8,128)(2,1)} copy(bf16[120,3584]{1,0:T(8,128)(2,1)} %get-tuple-element.4) | data formatting | bytes 1720320
  45.9 0.0 copy-done
  45.9 0.9 %copy.15 = bf16[120,3584]{1,0:T(8,128)(2,1)} copy(bf16[120,3584]{1,0:T(8,128)(2,1)S(1)} %copy-done) | data formatting | bytes 1720320
Async XLA Ops:
  43.7 2.2 %copy-start = (bf16[120,3584]{1,0:T(8,128)(2,1)S(1)}, bf16[120,3584]{1,0:T(8,128)(2,1)}, u32[]{:S(2)}) copy-start(bf16[120,3584]{1,0:T(8,128)(2,1)} %get-tuple-element.5) | copy-start | bytes 2580484

commit v3 on v2

--- a/solution.py
+++ b/solution.py
@@ -83,8 +83,6 @@
     partner = (section, expert + 1 - 2 * k)
 
     barrier = pltpu.get_barrier_semaphore()
-    pl.semaphore_signal(barrier, inc=1, device_id=partner, device_id_type=MESH)
-
     def greet(d, carry):
         pl.semaphore_signal(
             barrier, inc=1, device_id=device((me + d) % group), device_id_type=MESH
@@ -143,16 +141,27 @@
             cols = slice(part * chunk, (part + 1) * chunk)
             send_f[e, part] = jnp.dot(pick, x_ref[:, cols], preferred_element_type=F32).astype(BF16)
 
-    pl.semaphore_wait(barrier, group)
-    scatter(lambda n, e, part: send_f.at[e, part], in_f.at[me], inf_s, inf_r)
-    weight_copies = []
-    for i, ref in enumerate((gw_ref, uw_ref, dw_ref)):
-        copy = pltpu.make_async_remote_copy(
+    weight_copies = [
+        pltpu.make_async_remote_copy(
             src_ref=ref.at[0, 0], dst_ref=w.at[i, k], send_sem=w_s.at[i], recv_sem=w_r.at[i],
             device_id=partner, device_id_type=MESH,
         )
-        copy.start()
-        weight_copies.append(copy)
+        for i, ref in enumerate((gw_ref, uw_ref, dw_ref))
+    ]
+
+    @pl.when(k == 0)
+    def _():
+        pl.semaphore_wait(barrier, group - 1)
+        pl.semaphore_signal(barrier, inc=1, device_id=partner, device_id_type=MESH)
+
+    @pl.when(k == 1)
+    def _():
+        pl.semaphore_wait(barrier, group)
+        pl.semaphore_signal(barrier, inc=1, device_id=partner, device_id_type=MESH)
+        for copy in weight_copies:
+            copy.start()
+
+    scatter(lambda n, e, part: send_f.at[e, part], in_f.at[me], inf_s, inf_r)
 
     for copy in loads[2:6]:
         copy.wait()
@@ -167,6 +176,12 @@
             picked = jnp.dot(pick, g_ref[:, cols], preferred_element_type=F32)
             send_b[e, part, 1] = (picked * gate).astype(BF16)
     scatter(lambda n, e, part: send_b.at[e, part], in_b.at[me], inb_s, inb_r)
+
+    @pl.when(k == 0)
+    def _():
+        pl.semaphore_wait(barrier, 1)
+        for copy in weight_copies:
+            copy.start()
 
     in_f[me] = send_f[e_here, q]
     in_b[me] = send_b[e_here, q]

time: 47 us -> 46.4 us (0.987)
  Pallas kernels: 43 us -> 42.4 us
    pallas_call x1, Pallas kernels: 43 us -> 42.4 us  [per_device(): pl.pallas_call(functools.partial(kernel, n_expert, chunk), out_shape=(out...]
where the time goes in v3:
time: 46.4 us; the launch traced here: 46.2 us
  Pallas kernels  42.4 us (91%)
  local copies, waits for them, and re-layouts  3.1 us (7%)
  between operations  0.65 us (1%)
    pallas_call x1, Pallas kernels, per_device(): pl.pallas_call(functools.partial(kernel, n_expert, chunk), out_shape=(out...  42.4 us
    unnamed x4, local copies, waits for them, and re-layouts  3.1 us

profile of v3, /device:TPU:0, one launch (start us, length us, event | category | flops | bytes accessed | tf_op | source)
XLA Modules:
  0.0 46.2 jit_solution(536457511317936249)
XLA Ops:
  0.6 42.4 %shard_map.113 = (bf16[120,3584]{1,0:T(8,128)(2,1)}, bf16[120,3584]{1,0:T(8,128)(2,1)}) custom-call(bf16[120,3584]{1,0:T(8,128)(2,1)} %x_hbm.1, bf16[120,3584]{1,0:T(8,128)(2,1)} %s_hbm.1, bf16[120,3584]{1,0:T(8,128)(2,1)} %g_hbm.1, s32[8,120]{1,0:T(8,128)} %bitcast.4, f32[8,120]{1,0:T(8,128)} %bitcast.5, s32[8,120]{1,0:T(8,128)} %bitcast.6, ...), custom_call_target="tpu_custom_call" | custom-call | tf_op jit(solution)/shard_map/pallas_call | solution.py:346
  43.1 0.0 copy-start
  43.1 2.2 %copy.14 = bf16[120,3584]{1,0:T(8,128)(2,1)} copy(bf16[120,3584]{1,0:T(8,128)(2,1)} %get-tuple-element.4) | data formatting | bytes 1720320
  45.3 0.0 copy-done
  45.3 0.9 %copy.15 = bf16[120,3584]{1,0:T(8,128)(2,1)} copy(bf16[120,3584]{1,0:T(8,128)(2,1)S(1)} %copy-done) | data formatting | bytes 1720320
Async XLA Ops:
  43.1 2.2 %copy-start = (bf16[120,3584]{1,0:T(8,128)(2,1)S(1)}, bf16[120,3584]{1,0:T(8,128)(2,1)}, u32[]{:S(2)}) copy-start(bf16[120,3584]{1,0:T(8,128)(2,1)} %get-tuple-element.5) | copy-start | bytes 2580484

commit v4 on v3

--- a/solution.py
+++ b/solution.py
@@ -253,9 +253,8 @@
     scatter(lambda n, e, part: o_b.at[n], r_b.at[c, e_here, h, x], ob_s, ob_r)
     r_b[c, e_here, h, x] = o_b[me]
 
-    def combine(routes, gates, base, returned, out, out_hbm, weighted):
+    def picks_of(routes, gates, weighted):
         picks = []
-        stores = []
         for e in range(flight):
             tokens = routes.shape[1]
             chosen = chosen_of(routes[...], e, SLICES * CAP).astype(BF16)
@@ -267,6 +266,10 @@
                     NT, precision=lax.Precision.HIGHEST, preferred_element_type=F32,
                 )[:, :1]
             picks.append((chosen.astype(BF16), gate))
+        return picks
+
+    def combine(picks, base, returned, out, out_hbm, weighted):
+        stores = []
         for part in range(4):
             cols = slice(part * chunk, (part + 1) * chunk)
             total = base[:, cols].astype(F32)
@@ -286,17 +289,18 @@
     def slot_of(buffer):
         return lambda n: buffer.at[n // half, n % half // 8, n % half // 2 % 4, n % 2]
 
+    picks_f = picks_of(rf_ref, gf_ref, True)
+    picks_b = picks_of(rb_ref, gb_ref, False)
     gathered(o_f.at[0], slot_of(r_f), of_s, of_r)
-    stores = combine(rf_ref, gf_ref, x_ref, r_f, of_ref, of_hbm, True)
-    gathered(o_b.at[0], slot_of(r_b), ob_s, ob_r)
-    stores += combine(rb_ref, gb_ref, g_ref, r_b, ob_ref, ob_hbm, False)
-
+    stores = combine(picks_f, x_ref, r_f, of_ref, of_hbm, True)
     drained(send_f.at[0, 0], in_f.at[0], inf_s, inf_r)
     drained(send_b.at[0, 0], in_b.at[0], inb_s, inb_r)
     drained(o_f.at[0], r_f.at[0, 0, 0, 0], of_s, of_r)
-    drained(o_b.at[0], r_b.at[0, 0, 0, 0], ob_s, ob_r)
     for copy in weight_copies + sent_pf + sent_hf + sent_pb + sent_hb:
         copy.wait_send()
+    gathered(o_b.at[0], slot_of(r_b), ob_s, ob_r)
+    stores += combine(picks_b, g_ref, r_b, ob_ref, ob_hbm, False)
+    drained(o_b.at[0], r_b.at[0, 0, 0, 0], ob_s, ob_r)
     for copy in stores:
         copy.wait()
 

time: 46.4 us -> 46 us (level)
  no operation moved by 1% of the time
where the time goes in v4:
time: 46 us; the launch traced here: 45.8 us
  Pallas kernels  42 us (91%)
  local copies, waits for them, and re-layouts  3.1 us (7%)
  between operations  0.65 us (1%)
    pallas_call x1, Pallas kernels, per_device(): pl.pallas_call(functools.partial(kernel, n_expert, chunk), out_shape=(out...  42 us
    unnamed x4, local copies, waits for them, and re-layouts  3.1 us

profile of v4, /device:TPU:0, one launch (start us, length us, event | category | flops | bytes accessed | tf_op | source)
XLA Modules:
  0.0 45.8 jit_solution(15506257070551532665)
XLA Ops:
  0.6 42.0 %shard_map.113 = (bf16[120,3584]{1,0:T(8,128)(2,1)}, bf16[120,3584]{1,0:T(8,128)(2,1)}) custom-call(bf16[120,3584]{1,0:T(8,128)(2,1)} %x_hbm.1, bf16[120,3584]{1,0:T(8,128)(2,1)} %s_hbm.1, bf16[120,3584]{1,0:T(8,128)(2,1)} %g_hbm.1, s32[8,120]{1,0:T(8,128)} %bitcast.4, f32[8,120]{1,0:T(8,128)} %bitcast.5, s32[8,120]{1,0:T(8,128)} %bitcast.6, ...), custom_call_target="tpu_custom_call" | custom-call | tf_op jit(solution)/shard_map/pallas_call | solution.py:350
  42.7 0.0 copy-start
  42.7 2.2 %copy.14 = bf16[120,3584]{1,0:T(8,128)(2,1)} copy(bf16[120,3584]{1,0:T(8,128)(2,1)} %get-tuple-element.4) | data formatting | bytes 1720320
  44.9 0.0 copy-done
  44.9 0.9 %copy.15 = bf16[120,3584]{1,0:T(8,128)(2,1)} copy(bf16[120,3584]{1,0:T(8,128)(2,1)S(1)} %copy-done) | data formatting | bytes 1720320
Async XLA Ops:
  42.7 2.2 %copy-start = (bf16[120,3584]{1,0:T(8,128)(2,1)S(1)}, bf16[120,3584]{1,0:T(8,128)(2,1)}, u32[]{:S(2)}) copy-start(bf16[120,3584]{1,0:T(8,128)(2,1)} %get-tuple-element.5) | copy-start | bytes 2580484
